TPU v7x, 32 devices: a whole 2x2x4 slice. The times are simulated.
32 devices in a mesh: groups: 2 (over x), ta: 16 (over z, y, core).
Axes of the slice: x: 2, y: 2, z: 4, core: 2. Of those that a mesh axis runs over, the one named last changes fastest.
Arguments:
- gauge_links: float32 [4, 4, 256, 512], P(None, None, ('groups', 'ta')), parts along dimension 2, may hold values from -1 to 1, as said below
- cotangent: float32 [4, 4, 256, 512], P(None, None, ('groups', 'ta')), parts along dimension 2, may hold values from -6 to 6
- conv_weight: float32 [16, 243], replicated, may hold values from -0.375 to 0.375
- conv_bias: float32 [16], replicated, may hold values from -3 to 3
- head_weight: float32 [10, 16], replicated, may hold values from -1.5 to 1.5
- head_bias: float32 [10], replicated, may hold values from -3 to 3
- site_mask: int32 [256, 512], P(('groups', 'ta')), parts along dimension 0, may hold values from 0 to 1, as said below
- direction: int32 [4], replicated, may hold values from 0 to 3, each once
Outputs:
- grad_links: float32 [4, 4, 256, 512], P(None, None, ('groups', 'ta')), parts along dimension 2
- grad_conv_weight: float32 [32, 243], P('groups'), parts along dimension 0
- grad_conv_bias: float32 [32], P('groups'), parts along dimension 0
- grad_head_weight: float32 [20, 16], P('groups'), parts along dimension 0
- grad_head_bias: float32 [20], P('groups'), parts along dimension 0
There are 2 independent parts, one for each index of `groups`. A program takes and returns all parts, laid end to end along the dimension named above; an argument that names none is the same for every part. Nothing has to cross between parts.
Inputs may be any that keep to these rules, and one draw needn't show every extreme that they name: `gauge_links`: every link is a unit quaternion. `site_mask`: 1 only at sites whose coordinate sum t + x1 + x2 + x3 has one parity, the same over the whole lattice.
All inputs are finite; a program needn't handle non-finite values.
Results may differ from a plain program's by a relative error of at most 0.0003.
Values sent between devices are 32-bit elements; how exact they have to be, the bound alone decides.
A program may use at most 128 MiB of HBM per device.

v0:
```python
from functools import partial
import math

import jax
import jax.numpy as jnp
import numpy as np
from jax import lax
from jax.experimental import pallas as pl
from jax.experimental.pallas import tpu as pltpu
from jax.sharding import PartitionSpec as P

LS = 8
SITES = LS**3
OWN = 8
REACH = 3
ROWS = 16
HID = 16
FEAT = 3
COEF = 10
SPACE_TAPS = 27
GROUP = FEAT * ROWS
BANK = 1408
HIGH = lax.Precision.HIGHEST
NT = (((1,), (1,)), ((), ()))
TN = (((0,), (0,)), ((), ()))
NN = (((1,), (0,)), ((), ()))


def lane_roll(values, by):
    by = by % 128
    return jnp.concatenate(
        [pltpu.roll(values[:, at : at + 128], by, 1) for at in range(0, values.shape[1], 128)],
        axis=1,
    )


def moved(values, axis, offset):
    if axis == 0:
        return pltpu.roll(values, -offset % values.shape[0], 0)
    if axis == 1:
        return pltpu.roll(values, -offset * LS * LS % SITES, 1)
    stride = LS if axis == 2 else 1
    lane = lax.broadcasted_iota(jnp.int32, values.shape, 1)
    coordinate = (lane // stride) % LS
    wraps = coordinate == (LS - 1 if offset > 0 else 0)
    return jnp.where(
        wraps,
        lane_roll(values, offset * (LS - 1) * stride),
        lane_roll(values, -offset * stride),
    )


@partial(jax.custom_vjp, nondiff_argnums=(1, 2))
def shift(values, axis, offset):
    return moved(values, axis, offset)


shift.defvjp(
    lambda values, axis, offset: (moved(values, axis, offset), None),
    lambda axis, offset, _, grad: (moved(grad, axis, -offset),),
)


def q_shift(q, axis, offset):
    return tuple(shift(part, axis, offset) for part in q)


def q_mul(p, q):
    return (
        p[0] * q[0] - p[1] * q[1] - p[2] * q[2] - p[3] * q[3],
        p[0] * q[1] + p[1] * q[0] + p[2] * q[3] - p[3] * q[2],
        p[0] * q[2] - p[1] * q[3] + p[2] * q[0] + p[3] * q[1],
        p[0] * q[3] + p[1] * q[2] - p[2] * q[1] + p[3] * q[0],
    )


def q_conj(q):
    return (q[0], -q[1], -q[2], -q[3])


def staples(links, m):
    total = None
    for n in range(4):
        if n == m:
            continue
        ahead = q_shift(links[n], m, 1)
        upper = q_mul(q_mul(ahead, q_conj(q_shift(links[m], n, 1))), q_conj(links[n]))
        lower = q_shift(q_mul(q_conj(q_mul(links[m], ahead)), links[n]), n, -1)
        both = tuple(a + b for a, b in zip(upper, lower))
        total = both if total is None else tuple(a + b for a, b in zip(total, both))
    return total


def traces(links, m):
    others = [n for n in range(4) if n != m]
    out = []
    for i, j in ((0, 1), (0, 2), (1, 2)):
        a, b = others[i], others[j]
        left = q_mul(links[a], q_shift(links[b], a, 1))
        right = q_mul(links[b], q_shift(links[a], b, 1))
        out.append(sum(x * y for x, y in zip(left, right)))
    return tuple(out)


def cardinal(spot):
    rising = 0.5 * spot * spot
    middle = 0.5 * (-2.0 * spot * spot + 6.0 * spot - 3.0)
    falling = 0.5 * (3.0 - spot) * (3.0 - spot)
    return jnp.where(
        spot < 0.0,
        0.0,
        jnp.where(
            spot < 1.0, rising, jnp.where(spot < 2.0, middle, jnp.where(spot < 3.0, falling, 0.0))
        ),
    )


def rotate(link, staple, coeffs):
    loop = q_mul(link, staple)
    scaled = (loop[0] / 6.0 + 1.0) * (0.5 * (COEF - 2))
    strength = jnp.tanh(sum(coeffs[j] * cardinal(scaled - j + 2.0) for j in range(COEF)))
    turned = q_mul((jnp.zeros_like(loop[0]), loop[1], loop[2], loop[3]), link)
    length_sq = loop[1] * loop[1] + loop[2] * loop[2] + loop[3] * loop[3]
    scale = lax.rsqrt(1.0 + strength * strength * length_sq)
    return tuple((u + strength * v) * scale for u, v in zip(link, turned))


def halves(values):
    high = values.astype(jnp.bfloat16)
    return high, (values - high.astype(jnp.float32)).astype(jnp.bfloat16)


def dot3(a, b, dims):
    def one(x, y):
        return lax.dot_general(x, y, dims, preferred_element_type=jnp.float32)

    return one(a[0], b[0]) + (one(a[0], b[1]) + one(a[1], b[0]))


def group_roll(values, by):
    by = by % ROWS
    if by == 0:
        return values
    lane = lax.broadcasted_iota(jnp.int32, values.shape, 1) % ROWS
    return jnp.where(lane >= by, lane_roll(values, by), lane_roll(values, by - ROWS))


def kernel(
    m_ref, links_ref, halo_ref, cot_ref, mask_ref, w0_ref, head_ref, cb_ref, hb_ref,
    grad_ref, dw_ref, dcb_ref, dhw_ref, dhb_ref,
    feat_ref, staple_ref, link_ref, bank_hi, bank_lo, big_hi, big_lo, dbank_ref,
):
    m = m_ref[0]

    def load(d):
        return tuple(
            jnp.concatenate([links_ref[d, c], halo_ref[4 * d + c]], axis=0) for c in range(4)
        )

    for case in range(4):

        @pl.when(m == case)
        def _(case=case):
            links = tuple(load(d) for d in range(4))
            for k, value in enumerate(traces(links, case)):
                feat_ref[k * ROWS : (k + 1) * ROWS, :] = value
            for c, value in enumerate(staples(links, case)):
                staple_ref[c] = value

    w0 = w0_ref[...]
    for r in range(ROWS):
        high, low = halves(group_roll(w0, r))
        big_hi[r * HID : (r + 1) * HID, :] = high
        big_lo[r * HID : (r + 1) * HID, :] = low

    used = SPACE_TAPS * GROUP
    bank_hi[used:, :] = jnp.zeros((BANK - used, SITES), jnp.bfloat16)
    bank_lo[used:, :] = jnp.zeros((BANK - used, SITES), jnp.bfloat16)
    features = feat_ref[...]
    for c in (-1, 0, 1):
        third = moved(features, 3, c) if c else features
        for b in (-1, 0, 1):
            second = moved(third, 2, b) if b else third
            for a in (-1, 0, 1):
                first = moved(second, 1, a) if a else second
                e = ((a + 1) * 3 + b + 1) * 3 + c + 1
                high, low = halves(first)
                bank_hi[e * GROUP : (e + 1) * GROUP, :] = high
                bank_lo[e * GROUP : (e + 1) * GROUP, :] = low

    bank = (bank_hi[...], bank_lo[...])
    big = (big_hi[...], big_lo[...])
    hidden = jnp.tanh(dot3(big, bank, NN) + cb_ref[...])
    hidden2 = halves(hidden)
    head2 = halves(head_ref[...])
    coeffs = dot3(head2, hidden2, NN) + hb_ref[...]

    row = lax.broadcasted_iota(jnp.int32, (ROWS, SITES), 0)
    mask = jnp.concatenate([mask_ref[...], halo_ref[20]], axis=0)
    inside = (row <= OWN) | (row >= ROWS - 2)
    chosen = (mask != 0.0) & inside
    active = tuple(
        jnp.concatenate([links_ref[m, c], halo_ref[4 * m + c]], axis=0) for c in range(4)
    )
    cot = tuple(jnp.concatenate([cot_ref[m, c], halo_ref[16 + c]], axis=0) for c in range(4))
    _, pull = jax.vjp(
        rotate,
        active,
        tuple(staple_ref[c] for c in range(4)),
        tuple(coeffs[j * ROWS : (j + 1) * ROWS, :] for j in range(COEF)),
    )
    dlink, dstaple, dcoeff = pull(tuple(jnp.where(chosen, g, 0.0) for g in cot))
    for c in range(4):
        link_ref[c] = jnp.where(chosen, dlink[c], cot[c])[:OWN, :]
        staple_ref[c] = dstaple[c]
    dcoeff = jnp.concatenate(dcoeff, axis=0)
    dcoeff2 = halves(dcoeff)
    wide = lax.broadcasted_iota(jnp.int32, (COEF * ROWS, ROWS * HID), 1)
    tall = lax.broadcasted_iota(jnp.int32, (COEF * ROWS, ROWS * HID), 0)
    keep = (tall % ROWS == wide // HID) & (wide < OWN * HID)
    dhead = jnp.where(keep, dot3(dcoeff2, hidden2, NT), 0.0)
    fold = (
        lax.broadcasted_iota(jnp.int32, (ROWS * HID, 128), 0) % HID
        == lax.broadcasted_iota(jnp.int32, (ROWS * HID, 128), 1)
    ).astype(jnp.float32)
    folded = lax.dot_general(dhead, fold, NN, precision=HIGH, preferred_element_type=jnp.float32)
    dhw_ref[...] = jnp.concatenate(
        [jnp.sum(folded[j * ROWS : j * ROWS + OWN], axis=0, keepdims=True) for j in range(COEF)],
        axis=0,
    )
    own_sum = jnp.concatenate(
        [
            jnp.sum(dcoeff[j * ROWS : j * ROWS + OWN], axis=0, keepdims=True)
            for j in range(COEF)
        ],
        axis=0,
    )
    dhb_ref[...] = jnp.sum(own_sum, axis=1, keepdims=True)

    dpre = dot3(head2, dcoeff2, TN) * (1.0 - hidden * hidden)
    own_pre = dpre[: OWN * HID]
    pre_sum = sum(own_pre[r * HID : (r + 1) * HID] for r in range(OWN))
    dcb_ref[...] = jnp.sum(pre_sum, axis=1, keepdims=True)
    dpre2 = halves(dpre)
    dbig = dot3((dpre2[0][: OWN * HID], dpre2[1][: OWN * HID]), bank, NT)
    dw_ref[...] = sum(group_roll(dbig[r * HID : (r + 1) * HID], -r) for r in range(OWN))

    dbank_ref[...] = dot3(big, dpre2, TN)
    dfeat = None
    for c in (-1, 0, 1):
        third = None
        for b in (-1, 0, 1):
            second = None
            for a in (-1, 0, 1):
                e = ((a + 1) * 3 + b + 1) * 3 + c + 1
                part = dbank_ref[e * GROUP : (e + 1) * GROUP, :]
                part = moved(part, 1, -a) if a else part
                second = part if second is None else second + part
            second = moved(second, 2, -b) if b else second
            third = second if third is None else third + second
        third = moved(third, 3, -c) if c else third
        dfeat = third if dfeat is None else dfeat + third
    feat_ref[...] = dfeat

    for case in range(4):

        @pl.when(m == case)
        def _(case=case):
            links = tuple(load(d) for d in range(4))
            _, back = jax.vjp(lambda u: (traces(u, case), staples(u, case)), links)
            (dlinks,) = back(
                (
                    tuple(feat_ref[k * ROWS : (k + 1) * ROWS, :] for k in range(FEAT)),
                    tuple(staple_ref[c] for c in range(4)),
                )
            )
            for d in range(4):
                for c in range(4):
                    base = link_ref[c] if d == case else cot_ref[d, c]
                    grad_ref[d, c] = base + dlinks[d][c][:OWN, :]


def spread():
    table = np.zeros((3 * SPACE_TAPS * FEAT, BANK), np.float32)
    for a in range(3):
        for e in range(SPACE_TAPS):
            for k in range(FEAT):
                table[(a * SPACE_TAPS + e) * FEAT + k, e * GROUP + k * ROWS + (a - 1) % ROWS] = 1.0
    return table


def body(
    gauge_links, cotangent, conv_weight, conv_bias, head_weight, head_bias, site_mask, direction
):
    active = direction[0]
    mask = (site_mask != 0).astype(jnp.float32)
    active_cot = lax.dynamic_index_in_dim(cotangent, active, 0, keepdims=False)

    def message(rows):
        return jnp.concatenate(
            [
                gauge_links[:, :, rows].reshape(16, REACH, SITES),
                active_cot[:, rows],
                mask[None, rows],
            ],
            axis=0,
        )

    count = lax.axis_size("ta")
    ahead = lax.ppermute(
        message(slice(0, REACH)), "ta", [((i + 1) % count, i) for i in range(count)]
    )
    behind = lax.ppermute(
        message(slice(OWN - REACH, OWN)), "ta", [(i, (i + 1) % count) for i in range(count)]
    )
    halo = jnp.concatenate(
        [ahead, jnp.zeros((21, ROWS - OWN - 2 * REACH, SITES), jnp.float32), behind], axis=1
    )

    dropped = direction[jnp.array([3, 2, 1])]
    below = jnp.sum(
        (direction[1:][None, :] < dropped[:, None]).astype(jnp.int32), axis=1
    )
    perm = ((2 - below)[:, None] == jnp.arange(3)[None, :]).astype(jnp.float32)
    table = jnp.asarray(spread())
    sorted_weight = jnp.sum(
        conv_weight.reshape(HID, 3 * SPACE_TAPS, FEAT, 1) * perm[None, None], axis=2
    ).reshape(HID, 3 * SPACE_TAPS * FEAT)
    w0 = jnp.dot(sorted_weight, table, precision=HIGH)
    eye = jnp.eye(ROWS, dtype=jnp.float32)
    head = (head_weight[:, None, None, :] * eye[None, :, :, None]).reshape(
        COEF * ROWS, ROWS * HID
    )
    cb = jnp.tile(conv_bias, ROWS).reshape(ROWS * HID, 1)
    hb = jnp.repeat(head_bias, ROWS).reshape(COEF * ROWS, 1)

    vmem = pl.BlockSpec(memory_space=pltpu.VMEM)
    f32, bf16 = jnp.float32, jnp.bfloat16
    grad, dw0, dcb, dhw, dhb = pl.pallas_call(
        kernel,
        out_shape=(
            jax.ShapeDtypeStruct((4, 4, OWN, SITES), f32),
            jax.ShapeDtypeStruct((HID, BANK), f32),
            jax.ShapeDtypeStruct((HID, 1), f32),
            jax.ShapeDtypeStruct((COEF, 128), f32),
            jax.ShapeDtypeStruct((COEF, 1), f32),
        ),
        in_specs=[pl.BlockSpec(memory_space=pltpu.SMEM)] + [vmem] * 8,
        out_specs=(vmem,) * 5,
        scratch_shapes=[
            pltpu.VMEM((GROUP, SITES), f32),
            pltpu.VMEM((4, ROWS, SITES), f32),
            pltpu.VMEM((4, OWN, SITES), f32),
            pltpu.VMEM((BANK, SITES), bf16),
            pltpu.VMEM((BANK, SITES), bf16),
            pltpu.VMEM((ROWS * HID, BANK), bf16),
            pltpu.VMEM((ROWS * HID, BANK), bf16),
            pltpu.VMEM((BANK, SITES), f32),
        ],
        compiler_params=pltpu.CompilerParams(vmem_limit_bytes=40 * 2**20),
    )(direction, gauge_links, halo, cotangent, mask, w0, head, cb, hb)

    dweight = lax.dot_general(dw0, table, NT, precision=HIGH)
    summed = lax.psum((dweight, dcb[:, 0], dhw[:, :HID], dhb[:, 0]), "ta")
    dweight = jnp.sum(
        summed[0].reshape(HID, 3 * SPACE_TAPS, 1, FEAT) * perm[None, None], axis=3
    ).reshape(HID, 3 * SPACE_TAPS * FEAT)
    normalizer = 1.0 / math.sqrt(count * OWN * SITES)
    return (
        grad,
        dweight * normalizer,
        summed[1] * normalizer,
        summed[2] * normalizer,
        summed[3] * normalizer,
    )


def solution(mesh):
    return jax.shard_map(
        body,
        mesh=mesh,
        in_specs=(
            P(None, None, ("groups", "ta"), None),
            P(None, None, ("groups", "ta"), None),
            P(),
            P(),
            P(),
            P(),
            P(("groups", "ta"), None),
            P(),
        ),
        out_specs=(
            P(None, None, ("groups", "ta"), None),
            P("groups", None),
            P("groups"),
            P("groups", None),
            P("groups"),
        ),
        check_vma=False,
    )
```

profile of v0, /device:TPU:0, one launch (start us, length us, event | category | flops | bytes accessed | tf_op | source)
XLA Modules:
  0.0 96.5 jit_solution(3987874860401030832)
XLA Ops:
  2.7 0.8 dynamic-slice_bitcast_fusion
  3.5 0.7 compare_convert_fusion.mask_ref
  4.3 1.2 %fusion.2 = (f32[4,4,3,512]{3,2,1,0:T(4,128)S(1)}, f32[4,4,3,512]{3,2,1,0:T(4,128)S(1)}) fusion(f32[4,4,8,512]{3,2,1,0:T(8,128)} %links_ref.1), kind=kLoop, calls=%fused_computation.22 | loop fusion | bytes 393216 | tf_op jit(solution)/shard_map/slice | solution.py:302
  5.5 0.7 pad_maximum_fusion.1
  6.2 5.4 %collective-permute-start = (f32[21,3,512]{2,1,0:T(4,128)}, f32[21,3,512]{2,1,0:T(4,128)}, u32[]{:S(2)}, u32[]{:S(2)}) collective-permute-start(f32[21,3,512]{2,1,0:T(4,128)} %pad_maximum_fusion.1), channel_id=1, source_target_pairs={{1,0},{2,1},{3,2},{4,3},{5,4},{6,5},{7,6},{8,7},{9,8},{10,9},{11,1... | collective-permute-start | bytes 387080 | tf_op jit(solution)/shard_map/ppermute | solution.py:310
  11.6 0.7 pad_maximum_fusion.2
  12.4 0.6 gather_fusion
  13.1 0.2 convert_reduce_fusion
  13.3 0.1 copy.22
  13.5 0.1 copy.23
  13.6 0.1 multiply_reduce_fusion.1
  13.7 0.1 copy.24
  13.9 0.8 fusion.4.w0_ref
  14.7 0.2 broadcast_multiply_fusion
  14.9 0.6 mul.73.head_ref
  15.5 0.1 reshape_tile.4.cb_ref
  15.7 0.1 reshape_reshape.4.hb_ref
  15.8 0.1 pad.1.clone
  15.9 4.3 %collective-permute-done.1 = f32[21,3,512]{2,1,0:T(4,128)} collective-permute-done((f32[21,3,512]{2,1,0:T(4,128)}, f32[21,3,512]{2,1,0:T(4,128)}, u32[]{:S(2)}, u32[]{:S(2)}) %collective-permute-start.1) | collective-permute-done | bytes 129056 | tf_op jit(solution)/shard_map/ppermute | solution.py:313
  20.2 1.1 %pad_maximum_fusion.halo_ref = f32[21,8,512]{2,1,0:T(8,128)S(1)} fusion(f32[21,3,512]{2,1,0:T(4,128)} %collective-permute-done.1, f32[21,3,512]{2,1,0:T(4,128)} %collective-permute-done, f32[8]{0:T(128)S(1)} %pad.1.clone), kind=kLoop, calls=%fused_computation.2 | loop fusion | flops 172032 | bytes 602144 | tf_op jit(solution)/shard_map/concatenate | solution.py:316
  21.3 11.5 %shard_map.137 = (f32[4,4,8,512]{3,2,1,0:T(8,128)}, f32[16,1408]{1,0:T(8,128)S(1)}, f32[16,1]{1,0:T(8,128)S(1)}, f32[10,128]{1,0:T(8,128)S(1)}, f32[10,1]{1,0:T(8,128)S(1)}) custom-call(s32[4]{0:T(128)S(1)} %copy-done, f32[4,4,8,512]{3,2,1,0:T(8,128)S(1)} %copy-done.1, f32[21,8,512]{2,1,0:T(8,128)S(1)} %pad_maximum_fusion.halo_ref, ...), custom_call_target="tpu_custom_call" | custom-call | tf_op jit(solution)/shard_map/pallas_call | solution.py:339
  32.8 1.3 %fusion.5 = f32[16,243]{0,1:T(8,128)S(1)} fusion(f32[16,1408]{1,0:T(8,128)S(1)} %get-tuple-element.11, f32[243,1408]{1,0:T(8,128)S(1)} %copy-done.3), kind=kOutput, calls=%fused_computation.25 | convolution fusion | flops 65691648 | bytes 1474240 | tf_op jit(solution)/shard_map/dot_general | solution.py:363
  34.1 0.1 reduce
  34.3 0.1 reduce.1
  34.4 59.4 %all-reduce = (f32[16,81,3]{0,2,1:T(4,128)S(1)}, f32[16]{0:T(128)S(1)}, f32[10,16]{1,0:T(8,128)S(1)}, f32[10]{0:T(128)S(1)}) all-reduce(f32[16,81,3]{0,2,1:T(4,128)S(1)} %mul.74, f32[16]{0:T(128)S(1)} %reduce, f32[10,16]{1,0:T(8,128)S(1)} %bitcast.28, f32[10]{0:T(128)S(1)} %reduce.1), channel_id=1, replica_groups=mesh['groups'=2,'ta'=16] {'ta'}, use_global_device_ids=true, to_apply=%region_2.3 | all-reduce | flops 4074 | bytes 32592 | tf_op jit(solution)/shard_map/psum | solution.py:364
  93.8 0.1 copy.28
  93.8 0.1 multiply_reduce_fusion
  94.0 0.1 copy.29
  94.2 0.7 copy.30
  94.8 0.6 broadcast_multiply_fusion.2
  95.4 0.5 broadcast_multiply_fusion.3
  96.0 0.5 broadcast_multiply_fusion.4
  (35 shorter events, 0.5 us)
Async XLA Ops:
  0.6 11.8 %copy-start.8 = (s32[3]{0:T(128)S(1)}, s32[3]{0:T(128)}, u32[]{:S(2)}) copy-start(s32[3]{0:T(128)} %constant.33) | copy-start | bytes 40
  0.6 11.7 %copy-start = (s32[4]{0:T(128)S(1)}, s32[4]{0:T(128)}, u32[]{:S(2)}) copy-start(s32[4]{0:T(128)} %m_ref.1) | copy-start | bytes 52
  0.7 12.7 %copy-start.4 = (f32[16,243]{1,0:T(8,128)S(1)}, f32[16,243]{1,0:T(8,128)}, u32[]{:S(2)}) copy-start(f32[16,243]{1,0:T(8,128)} %param.12) | copy-start | bytes 46660
  4.3 9.6 %copy-start.3 = (f32[243,1408]{1,0:T(8,128)S(1)}, f32[243,1408]{1,0:T(8,128)}, u32[]{:S(2)}) copy-start(f32[243,1408]{1,0:T(8,128)} %constant.13.clone) | copy-start | bytes 4105732
  6.2 9.7 %collective-permute-start = (f32[21,3,512]{2,1,0:T(4,128)}, f32[21,3,512]{2,1,0:T(4,128)}, u32[]{:S(2)}, u32[]{:S(2)}) collective-permute-start(f32[21,3,512]{2,1,0:T(4,128)} %pad_maximum_fusion.1), channel_id=1, source_target_pairs={{1,0},{2,1},{3,2},{4,3},{5,4},{6,5},{7,6},{8,7},{9,8},{10,9},{11,1... | collective-permute-start | bytes 387080 | tf_op jit(solution)/shard_map/ppermute | solution.py:310
  12.3 7.8 %collective-permute-start.1 = (f32[21,3,512]{2,1,0:T(4,128)}, f32[21,3,512]{2,1,0:T(4,128)}, u32[]{:S(2)}, u32[]{:S(2)}) collective-permute-start(f32[21,3,512]{2,1,0:T(4,128)} %pad_maximum_fusion.2), channel_id=1, source_target_pairs={{0,1},{1,2},{2,3},{3,4},{4,5},{5,6},{6,7},{7,8},{8,9},{9,10},{10,1... | collective-permute-start | bytes 387080 | tf_op jit(solution)/shard_map/ppermute | solution.py:313
  13.1 1.7 %copy-start.5 = (f32[10,16]{1,0:T(8,128)S(1)}, f32[10,16]{1,0:T(8,128)}, u32[]{:S(2)}) copy-start(f32[10,16]{1,0:T(8,128)} %param.14) | copy-start | bytes 1924
  14.7 0.8 copy-start.6
  14.7 0.9 copy-start.7
  14.9 6.4 %copy-start.1 = (f32[4,4,8,512]{3,2,1,0:T(8,128)S(1)}, f32[4,4,8,512]{3,2,1,0:T(8,128)}, u32[]{:S(2)}) copy-start(f32[4,4,8,512]{3,2,1,0:T(8,128)} %links_ref.1) | copy-start | bytes 786436
  14.9 6.4 %copy-start.2 = (f32[4,4,8,512]{3,2,1,0:T(8,128)S(1)}, f32[4,4,8,512]{3,2,1,0:T(8,128)}, u32[]{:S(2)}) copy-start(f32[4,4,8,512]{3,2,1,0:T(8,128)} %cot_ref.1) | copy-start | bytes 786436
where the time goes:
time: 96.8 us; the launch traced here: 96.5 us
  blocking collectives  59.4 us (61%)
  Pallas kernels  11.5 us (12%)
  other arithmetic  5.72 us (6%)
  starting transfers between devices  5.45 us (6%)
  local copies, waits for them, and re-layouts  5.19 us (5%)
  waiting for transfers between devices  4.26 us (4%)
  between operations  2.88 us (3%)
  matrix products  2.14 us (2%)
    psum x1, blocking collectives, body(): summed = lax.psum((dweight, dcb[:, 0], dhw[:, :HID], dhb[:, 0]), 'ta')  59.4 us
    pallas_call x1, Pallas kernels, body(): pl.pallas_call(kernel, out_shape=(jax.ShapeDtypeStruct((4, 4, OWN, SITES)...  11.5 us
    ppermute x1, starting transfers between devices, body(): lax.ppermute(message(slice(0, REACH)), 'ta', [((i + 1) % count, i) for i...  5.44 us
    ppermute x1, waiting for transfers between devices, body(): lax.ppermute(message(slice(OWN - REACH, OWN)), 'ta', [(i, (i + 1) % count...  4.26 us
  transfers between devices with their start and end apart: 2, of which 1 were waited for; matrix products, arithmetic and copies ran while one was open for 4% of the time, Pallas kernels for 0%

commit v1 on v0

--- a/solution.py
+++ b/solution.py
@@ -20,6 +20,10 @@
 SPACE_TAPS = 27
 GROUP = FEAT * ROWS
 BANK = 1408
+AT_CB = 3 * SPACE_TAPS * FEAT
+AT_HEAD = AT_CB + 1
+AT_HB = AT_HEAD + COEF
+PACK = 256
 HIGH = lax.Precision.HIGHEST
 NT = (((1,), (1,)), ((), ()))
 TN = (((0,), (0,)), ((), ()))
@@ -146,8 +150,8 @@
 
 
 def kernel(
-    m_ref, links_ref, halo_ref, cot_ref, mask_ref, w0_ref, head_ref, cb_ref, hb_ref,
-    grad_ref, dw_ref, dcb_ref, dhw_ref, dhb_ref,
+    scale, m_ref, links_ref, halo_ref, cot_ref, mask_ref, cw_ref, table_ref, head_ref, cb_ref,
+    hb_ref, grad_ref, pack_ref,
     feat_ref, staple_ref, link_ref, bank_hi, bank_lo, big_hi, big_lo, dbank_ref,
 ):
     m = m_ref[0]
@@ -157,17 +161,27 @@
             jnp.concatenate([links_ref[d, c], halo_ref[4 * d + c]], axis=0) for c in range(4)
         )
 
+    def slots(case):
+        others = [n for n in range(4) if n != case]
+        found = []
+        for missing in reversed(others):
+            k = jnp.where(m_ref[3] == missing, 0, jnp.where(m_ref[2] == missing, 1, 2))
+            found.append(pl.ds(pl.multiple_of(k * ROWS, ROWS), ROWS))
+        return found
+
     for case in range(4):
 
         @pl.when(m == case)
         def _(case=case):
             links = tuple(load(d) for d in range(4))
-            for k, value in enumerate(traces(links, case)):
-                feat_ref[k * ROWS : (k + 1) * ROWS, :] = value
+            for at, value in zip(slots(case), traces(links, case)):
+                feat_ref[at, :] = value
             for c, value in enumerate(staples(links, case)):
                 staple_ref[c] = value
 
-    w0 = w0_ref[...]
+    w0 = lax.dot_general(
+        cw_ref[...], table_ref[...], NN, precision=HIGH, preferred_element_type=jnp.float32
+    )
     for r in range(ROWS):
         high, low = halves(group_roll(w0, r))
         big_hi[r * HID : (r + 1) * HID, :] = high
@@ -215,35 +229,39 @@
         staple_ref[c] = dstaple[c]
     dcoeff = jnp.concatenate(dcoeff, axis=0)
     dcoeff2 = halves(dcoeff)
-    wide = lax.broadcasted_iota(jnp.int32, (COEF * ROWS, ROWS * HID), 1)
-    tall = lax.broadcasted_iota(jnp.int32, (COEF * ROWS, ROWS * HID), 0)
-    keep = (tall % ROWS == wide // HID) & (wide < OWN * HID)
-    dhead = jnp.where(keep, dot3(dcoeff2, hidden2, NT), 0.0)
+    wide = lax.broadcasted_iota(jnp.int32, (ROWS * HID, COEF * ROWS), 1)
+    tall = lax.broadcasted_iota(jnp.int32, (ROWS * HID, COEF * ROWS), 0)
+    keep = (wide % ROWS == tall // HID) & (tall < OWN * HID)
+    dhead = jnp.where(keep, dot3(hidden2, dcoeff2, NT), 0.0)
+    dhead = sum(dhead[r * HID : (r + 1) * HID] for r in range(OWN))
     fold = (
-        lax.broadcasted_iota(jnp.int32, (ROWS * HID, 128), 0) % HID
-        == lax.broadcasted_iota(jnp.int32, (ROWS * HID, 128), 1)
+        lax.broadcasted_iota(jnp.int32, (COEF * ROWS, 128), 0) // ROWS + (AT_HEAD - 128)
+        == lax.broadcasted_iota(jnp.int32, (COEF * ROWS, 128), 1)
     ).astype(jnp.float32)
-    folded = lax.dot_general(dhead, fold, NN, precision=HIGH, preferred_element_type=jnp.float32)
-    dhw_ref[...] = jnp.concatenate(
-        [jnp.sum(folded[j * ROWS : j * ROWS + OWN], axis=0, keepdims=True) for j in range(COEF)],
-        axis=0,
-    )
+    extra = lax.dot_general(dhead, fold, NN, precision=HIGH, preferred_element_type=jnp.float32)
     own_sum = jnp.concatenate(
         [
             jnp.sum(dcoeff[j * ROWS : j * ROWS + OWN], axis=0, keepdims=True)
             for j in range(COEF)
-        ],
+        ]
+        + [jnp.zeros((HID - COEF, SITES), jnp.float32)],
         axis=0,
     )
-    dhb_ref[...] = jnp.sum(own_sum, axis=1, keepdims=True)
+    column = lax.broadcasted_iota(jnp.int32, (HID, 128), 1)
+    extra += jnp.where(column == AT_HB - 128, jnp.sum(own_sum, axis=1, keepdims=True), 0.0)
 
     dpre = dot3(head2, dcoeff2, TN) * (1.0 - hidden * hidden)
     own_pre = dpre[: OWN * HID]
     pre_sum = sum(own_pre[r * HID : (r + 1) * HID] for r in range(OWN))
-    dcb_ref[...] = jnp.sum(pre_sum, axis=1, keepdims=True)
+    extra += jnp.where(column == AT_CB - 128, jnp.sum(pre_sum, axis=1, keepdims=True), 0.0)
     dpre2 = halves(dpre)
     dbig = dot3((dpre2[0][: OWN * HID], dpre2[1][: OWN * HID]), bank, NT)
-    dw_ref[...] = sum(group_roll(dbig[r * HID : (r + 1) * HID], -r) for r in range(OWN))
+    dw0 = sum(group_roll(dbig[r * HID : (r + 1) * HID], -r) for r in range(OWN))
+    dw = lax.dot_general(
+        dw0, table_ref[...], NT, precision=HIGH, preferred_element_type=jnp.float32
+    )
+    pack_ref[:, :128] = dw[:, :128] * scale
+    pack_ref[:, 128:] = (dw[:, 128:] + extra) * scale
 
     dbank_ref[...] = dot3(big, dpre2, TN)
     dfeat = None
@@ -270,7 +288,7 @@
             _, back = jax.vjp(lambda u: (traces(u, case), staples(u, case)), links)
             (dlinks,) = back(
                 (
-                    tuple(feat_ref[k * ROWS : (k + 1) * ROWS, :] for k in range(FEAT)),
+                    tuple(feat_ref[at, :] for at in slots(case)),
                     tuple(staple_ref[c] for c in range(4)),
                 )
             )
@@ -281,12 +299,69 @@
 
 
 def spread():
-    table = np.zeros((3 * SPACE_TAPS * FEAT, BANK), np.float32)
+    table = np.zeros((PACK, BANK), np.float32)
     for a in range(3):
         for e in range(SPACE_TAPS):
             for k in range(FEAT):
                 table[(a * SPACE_TAPS + e) * FEAT + k, e * GROUP + k * ROWS + (a - 1) % ROWS] = 1.0
     return table
+
+
+def sum_kernel(
+    n, x_ref, out_ref, parts_ref, sums_ref, mine_ref, send1, recv1, send2, recv2
+):
+    me = lax.axis_index("ta")
+    mesh_id = pl.DeviceIdType.MESH
+
+    def to(k):
+        return lax.rem(me + k, n)
+
+    def scatter(k):
+        return pltpu.make_async_remote_copy(
+            src_ref=x_ref.at[to(k)],
+            dst_ref=parts_ref.at[k],
+            send_sem=send1.at[k],
+            recv_sem=recv1.at[k],
+            device_id={"ta": to(k)},
+            device_id_type=mesh_id,
+        )
+
+    def gather(k):
+        return pltpu.make_async_remote_copy(
+            src_ref=mine_ref,
+            dst_ref=sums_ref.at[k],
+            send_sem=send2.at[k],
+            recv_sem=recv2.at[k],
+            device_id={"ta": to(k)},
+            device_id_type=mesh_id,
+        )
+
+    def each(act):
+        lax.fori_loop(1, n, lambda k, carry: (act(k), carry)[1], 0)
+
+    barrier = pltpu.get_barrier_semaphore()
+    each(
+        lambda k: pl.semaphore_signal(
+            barrier, inc=1, device_id={"ta": to(k)}, device_id_type=mesh_id
+        )
+    )
+    pl.semaphore_wait(barrier, n - 1)
+    each(lambda k: scatter(k).start())
+    each(lambda k: scatter(k).wait_recv())
+    total = x_ref[me]
+    for k in range(1, n):
+        total = total + parts_ref[k]
+    mine_ref[...] = total
+    each(lambda k: gather(k).start())
+    out_ref[me] = total
+
+    def keep(k):
+        gather(k).wait_recv()
+        out_ref[lax.rem(me + n - k, n)] = sums_ref[k]
+
+    each(keep)
+    each(lambda k: scatter(k).wait_send())
+    each(lambda k: gather(k).wait_send())
 
 
 def body(
@@ -317,16 +392,8 @@
         [ahead, jnp.zeros((21, ROWS - OWN - 2 * REACH, SITES), jnp.float32), behind], axis=1
     )
 
-    dropped = direction[jnp.array([3, 2, 1])]
-    below = jnp.sum(
-        (direction[1:][None, :] < dropped[:, None]).astype(jnp.int32), axis=1
-    )
-    perm = ((2 - below)[:, None] == jnp.arange(3)[None, :]).astype(jnp.float32)
     table = jnp.asarray(spread())
-    sorted_weight = jnp.sum(
-        conv_weight.reshape(HID, 3 * SPACE_TAPS, FEAT, 1) * perm[None, None], axis=2
-    ).reshape(HID, 3 * SPACE_TAPS * FEAT)
-    w0 = jnp.dot(sorted_weight, table, precision=HIGH)
+    weight = jnp.pad(conv_weight, ((0, 0), (0, PACK - AT_CB)))
     eye = jnp.eye(ROWS, dtype=jnp.float32)
     head = (head_weight[:, None, None, :] * eye[None, :, :, None]).reshape(
         COEF * ROWS, ROWS * HID
@@ -336,17 +403,14 @@
 
     vmem = pl.BlockSpec(memory_space=pltpu.VMEM)
     f32, bf16 = jnp.float32, jnp.bfloat16
-    grad, dw0, dcb, dhw, dhb = pl.pallas_call(
-        kernel,
+    grad, packed = pl.pallas_call(
+        partial(kernel, 1.0 / math.sqrt(count * OWN * SITES)),
         out_shape=(
             jax.ShapeDtypeStruct((4, 4, OWN, SITES), f32),
-            jax.ShapeDtypeStruct((HID, BANK), f32),
-            jax.ShapeDtypeStruct((HID, 1), f32),
-            jax.ShapeDtypeStruct((COEF, 128), f32),
-            jax.ShapeDtypeStruct((COEF, 1), f32),
+            jax.ShapeDtypeStruct((HID, PACK), f32),
         ),
-        in_specs=[pl.BlockSpec(memory_space=pltpu.SMEM)] + [vmem] * 8,
-        out_specs=(vmem,) * 5,
+        in_specs=[pl.BlockSpec(memory_space=pltpu.SMEM)] + [vmem] * 9,
+        out_specs=(vmem,) * 2,
         scratch_shapes=[
             pltpu.VMEM((GROUP, SITES), f32),
             pltpu.VMEM((4, ROWS, SITES), f32),
@@ -358,20 +422,28 @@
             pltpu.VMEM((BANK, SITES), f32),
         ],
         compiler_params=pltpu.CompilerParams(vmem_limit_bytes=40 * 2**20),
-    )(direction, gauge_links, halo, cotangent, mask, w0, head, cb, hb)
-
-    dweight = lax.dot_general(dw0, table, NT, precision=HIGH)
-    summed = lax.psum((dweight, dcb[:, 0], dhw[:, :HID], dhb[:, 0]), "ta")
-    dweight = jnp.sum(
-        summed[0].reshape(HID, 3 * SPACE_TAPS, 1, FEAT) * perm[None, None], axis=3
-    ).reshape(HID, 3 * SPACE_TAPS * FEAT)
-    normalizer = 1.0 / math.sqrt(count * OWN * SITES)
+    )(direction, gauge_links, halo, cotangent, mask, weight, table, head, cb, hb)
+
+    depth = -(-HID // count)
+    packed = jnp.pad(packed, ((0, count * depth - HID), (0, 0)))
+    shape = (count, depth, PACK)
+    summed = pl.pallas_call(
+        partial(sum_kernel, count),
+        out_shape=jax.ShapeDtypeStruct(shape, f32),
+        in_specs=[vmem],
+        out_specs=vmem,
+        scratch_shapes=[pltpu.VMEM(shape, f32)] * 2
+        + [pltpu.VMEM((depth, PACK), f32)]
+        + [pltpu.SemaphoreType.DMA((count,))] * 4,
+        compiler_params=pltpu.CompilerParams(collective_id=0, has_side_effects=True),
+    )(packed.reshape(shape))
+    summed = summed.reshape(count * depth, PACK)[:HID]
     return (
         grad,
-        dweight * normalizer,
-        summed[1] * normalizer,
-        summed[2] * normalizer,
-        summed[3] * normalizer,
+        summed[:, :AT_CB],
+        summed[:, AT_CB],
+        summed[:, AT_HEAD:AT_HB].T,
+        summed[:COEF, AT_HB],
     )
 
 

time: 96.8 us -> 48.9 us (0.51)
  blocking collectives: 59.4 us -> 0 us
  Pallas kernels: 11.5 us -> 23.8 us
  waiting for transfers between devices: 4.26 us -> 6.58 us
  other arithmetic: 5.72 us -> 3.42 us
  matrix products: 2.14 us -> 0 us
  local copies, waits for them, and re-layouts: 5.19 us -> 6.38 us
    psum x1 -> x0, blocking collectives: 59.4 us -> none  [body(): summed = lax.psum((dweight, dcb[:, 0], dhw[:, :HID], dhb[:, 0]), 'ta')]
    pallas_call x1 -> x2, Pallas kernels: 11.5 us -> 23.8 us  [the longest x1 13.1 us: body(): pl.pallas_call(partial(kernel, 1.0 / math.sqrt(count * OWN * SITES)), out...]
    dot_general x2 -> x0, matrix products: 2.14 us -> none  [the longest x1 1.32 us: body(): dweight = lax.dot_general(dw0, table, NT, precision=HIGH)]
    mul x4 -> x0, other arithmetic: 1.63 us -> none  [the longest x1 0.6 us: body(): summed[2] * normalizer]
    slice x1 -> x2, local copies, waits for them, and re-layouts: 0.07 us -> 1.39 us  [the longest x1 0.69 us: body(): summed[:COEF, AT_HB]]
    ppermute x1, waiting for transfers between devices: 0.01 us -> 1.27 us  [body(): lax.ppermute(message(slice(0, REACH)), 'ta', [((i + 1) % count, i) for i...]
    ppermute x1, waiting for transfers between devices: 4.26 us -> 5.31 us  [body(): lax.ppermute(message(slice(OWN - REACH, OWN)), 'ta', [(i, (i + 1) % count...]
  transfers between devices with their start and end apart: 2 -> 2, of which waited for: 1 -> 2; matrix products, arithmetic and copies ran while one was open for 4% -> 4% of each run, Pallas kernels for 0% -> 0%
where the time goes in v1:
time: 48.9 us; the launch traced here: 48.4 us
  Pallas kernels  23.8 us (49%)
  waiting for transfers between devices  6.58 us (13%)
  local copies, waits for them, and re-layouts  6.38 us (13%)
  starting transfers between devices  5.45 us (11%)
  other arithmetic  3.42 us (7%)
  between operations  2.78 us (6%)
    pallas_call x1, Pallas kernels, body(): pl.pallas_call(partial(kernel, 1.0 / math.sqrt(count * OWN * SITES)), out...  13.1 us
    pallas_call x1, Pallas kernels, body(): pl.pallas_call(partial(sum_kernel, count), out_shape=jax.ShapeDtypeStruct...  10.7 us
    ppermute x1, starting transfers between devices, body(): lax.ppermute(message(slice(0, REACH)), 'ta', [((i + 1) % count, i) for i...  5.44 us
    ppermute x1, waiting for transfers between devices, body(): lax.ppermute(message(slice(OWN - REACH, OWN)), 'ta', [(i, (i + 1) % count...  5.31 us
    unnamed x20, local copies, waits for them, and re-layouts  1.45 us
    concatenate x2, other arithmetic, message(): jnp.concatenate([gauge_links[:, :, rows].reshape(16, REACH, SITES), activ...  1.41 us
    ppermute x1, waiting for transfers between devices, body(): lax.ppermute(message(slice(0, REACH)), 'ta', [((i + 1) % count, i) for i...  1.27 us
    concatenate x1, other arithmetic, body(): jnp.concatenate([ahead, jnp.zeros((21, ROWS - OWN - 2 * REACH, SITES), jn...  1.11 us
  transfers between devices with their start and end apart: 2, of which 2 were waited for; matrix products, arithmetic and copies ran while one was open for 4% of the time, Pallas kernels for 0%

profile of v1, /device:TPU:0, one launch (start us, length us, event | category | flops | bytes accessed | tf_op | source)
XLA Modules:
  0.0 48.4 jit_solution(401308596278371799)
XLA Ops:
  2.6 0.8 %dynamic-slice_bitcast_fusion = f32[4,8,512]{2,1,0:T(8,128)S(1)} fusion(f32[4,4,8,512]{3,2,1,0:T(8,128)} %cot_ref.1, s32[]{:T(128)S(6)} %select_n.4), kind=kLoop, calls=%fused_computation.4 | loop fusion | bytes 131076 | tf_op jit(solution)/shard_map/jit(dynamic_index_in_dim)/squeeze | solution.py:372
  3.5 0.7 %compare_convert_fusion.mask_ref = f32[8,512]{1,0:T(8,128)S(1)} fusion(s32[8,512]{1,0:T(8,128)} %param.15), kind=kLoop, calls=%fused_computation.6 | loop fusion | flops 8192 | bytes 32768 | tf_op jit(solution)/shard_map/convert_element_type | solution.py:371
  4.2 1.1 %fusion.1 = (f32[4,4,3,512]{3,2,1,0:T(4,128)S(1)}, f32[4,4,3,512]{3,2,1,0:T(4,128)S(1)}) fusion(f32[4,4,8,512]{3,2,1,0:T(8,128)} %links_ref.1), kind=kLoop, calls=%fused_computation.14 | loop fusion | bytes 393216 | tf_op jit(solution)/shard_map/slice | solution.py:377
  5.3 0.7 %pad_maximum_fusion.1 = f32[21,3,512]{2,1,0:T(4,128)} fusion(f32[1,3,512]{2,1,0:T(4,128)S(1)} %get-tuple-element.23, f32[4,3,512]{2,1,0:T(4,128)S(1)} %get-tuple-element.21, f32[16,3,512]{2,1,0:T(4,128)S(1)} %bitcast.22), kind=kLoop, calls=%fused_computation.2 | loop fusion | flops 64512 | bytes 258048 | tf_op jit(solution)/shard_map/concatenate | solution.py:375
  6.0 5.4 %collective-permute-start = (f32[21,3,512]{2,1,0:T(4,128)}, f32[21,3,512]{2,1,0:T(4,128)}, u32[]{:S(2)}, u32[]{:S(2)}) collective-permute-start(f32[21,3,512]{2,1,0:T(4,128)} %pad_maximum_fusion.1), channel_id=1, source_target_pairs={{1,0},{2,1},{3,2},{4,3},{5,4},{6,5},{7,6},{8,7},{9,8},{10,9},{11,1... | collective-permute-start | bytes 387080 | tf_op jit(solution)/shard_map/ppermute | solution.py:385
  11.4 0.7 %pad_maximum_fusion.2 = f32[21,3,512]{2,1,0:T(4,128)} fusion(f32[1,3,512]{2,1,0:T(4,128)S(1)} %get-tuple-element.24, f32[4,3,512]{2,1,0:T(4,128)S(1)} %get-tuple-element.22, f32[16,3,512]{2,1,0:T(4,128)S(1)} %bitcast.21), kind=kLoop, calls=%fused_computation.3 | loop fusion | flops 64512 | bytes 258048 | tf_op jit(solution)/shard_map/concatenate | solution.py:375
  12.1 0.0 collective-permute-start.1
  12.1 0.0 copy-start.7
  12.1 0.0 copy-start.8
  12.2 0.0 copy-start.5
  12.2 0.2 broadcast_multiply_fusion
  12.4 0.0 copy-start
  12.4 0.0 copy-start.1
  12.4 0.0 copy-start.2
  12.4 0.0 copy-start.3
  12.4 0.6 %mul.20.head_ref = f32[160,256]{1,0:T(8,128)S(1)} reshape(f32[10,16,16,16]{3,2,1,0:T(8,128)S(1)} %broadcast_multiply_fusion) | data formatting | bytes 327680 | tf_op jit(solution)/shard_map/mul | solution.py:398
  13.0 0.1 reshape_tile.4.cb_ref
  13.1 0.0 copy-done.8
  13.1 0.1 broadcast_in_dim.17
  13.2 0.1 reshape_reshape.4.hb_ref
  13.3 0.1 pad.6.clone
  13.4 1.3 %collective-permute-done = f32[21,3,512]{2,1,0:T(4,128)} collective-permute-done((f32[21,3,512]{2,1,0:T(4,128)}, f32[21,3,512]{2,1,0:T(4,128)}, u32[]{:S(2)}, u32[]{:S(2)}) %collective-permute-start) | collective-permute-done | bytes 129056 | tf_op jit(solution)/shard_map/ppermute | solution.py:385
  14.7 5.3 %collective-permute-done.1 = f32[21,3,512]{2,1,0:T(4,128)} collective-permute-done((f32[21,3,512]{2,1,0:T(4,128)}, f32[21,3,512]{2,1,0:T(4,128)}, u32[]{:S(2)}, u32[]{:S(2)}) %collective-permute-start.1) | collective-permute-done | bytes 129056 | tf_op jit(solution)/shard_map/ppermute | solution.py:388
  20.0 1.1 %pad_maximum_fusion.halo_ref = f32[21,8,512]{2,1,0:T(8,128)S(1)} fusion(f32[21,3,512]{2,1,0:T(4,128)} %collective-permute-done.1, f32[21,3,512]{2,1,0:T(4,128)} %collective-permute-done, f32[8]{0:T(128)S(1)} %pad.6.clone), kind=kLoop, calls=%fused_computation.1 | loop fusion | flops 172032 | bytes 602144 | tf_op jit(solution)/shard_map/concatenate | solution.py:391
  21.1 13.1 %shard_map.128 = (f32[4,4,8,512]{3,2,1,0:T(8,128)}, f32[16,256]{1,0:T(8,128)S(1)}) custom-call(s32[4]{0:T(128)S(1)} %copy-done.3, f32[4,4,8,512]{3,2,1,0:T(8,128)S(1)} %copy-done.1, f32[21,8,512]{2,1,0:T(8,128)S(1)} %pad_maximum_fusion.halo_ref, f32[4,4,8,512]{3,2,1,0:T(8,128)S(1)} %copy-done.2, f32[8,512]{1,0:T(8,128)S(1)} %compare_convert_fusion.mask_ref, ...), custom_call_target="tpu_custom_call" | custom-call | tf_op jit(solution)/shard_map/pallas_call | solution.py:406
  34.2 0.6 %reshape.38.x_ref = f32[16,1,256]{2,1,0:T(1,128)} reshape(f32[16,256]{1,0:T(8,128)S(1)} %get-tuple-element.8) | data formatting | bytes 32768 | tf_op jit(solution)/shard_map/reshape | solution.py:439
  34.8 10.7 %shard_map.129 = f32[16,1,256]{2,1,0:T(1,128)} custom-call(f32[16,1,256]{2,1,0:T(1,128)} %reshape.38.x_ref), custom_call_target="tpu_custom_call" | custom-call | tf_op jit(solution)/shard_map/pallas_call | solution.py:430
  45.5 0.7 %copy.20 = f32[16,1,256]{2,0,1:T(8,128)S(1)} copy(f32[16,1,256]{2,1,0:T(1,128)} %shard_map.129) | data formatting | bytes 32768
  46.3 0.1 slice_bitcast_fusion
  46.3 0.7 %slice_reduce_fusion = f32[10]{0:T(128)} fusion(f32[16,256]{1,0:T(8,128)S(1)} %bitcast.24), kind=kLoop, calls=%fused_computation.7 | loop fusion | bytes 80 | tf_op jit(solution)/shard_map/slice | solution.py:446
  47.0 0.7 %slice_reduce_fusion.1 = f32[16]{0:T(128)} fusion(f32[16,256]{1,0:T(8,128)S(1)} %bitcast.25), kind=kLoop, calls=%fused_computation.9 | loop fusion | bytes 128 | tf_op jit(solution)/shard_map/slice | solution.py:444
  47.7 0.7 %copy.17 = f32[10,16]{1,0:T(8,128)} copy(f32[10,16]{0,1:T(8,128)S(1)} %slice_bitcast_fusion) | data formatting | bytes 1280
  (16 shorter events, 0.1 us)
Async XLA Ops:
  0.6 11.5 %copy-start.6 = (f32[10,16]{1,0:T(8,128)S(1)}, f32[10,16]{1,0:T(8,128)}, u32[]{:S(2)}) copy-start(f32[10,16]{1,0:T(8,128)} %param.13) | copy-start | bytes 1924
  6.0 8.7 %collective-permute-start = (f32[21,3,512]{2,1,0:T(4,128)}, f32[21,3,512]{2,1,0:T(4,128)}, u32[]{:S(2)}, u32[]{:S(2)}) collective-permute-start(f32[21,3,512]{2,1,0:T(4,128)} %pad_maximum_fusion.1), channel_id=1, source_target_pairs={{1,0},{2,1},{3,2},{4,3},{5,4},{6,5},{7,6},{8,7},{9,8},{10,9},{11,1... | collective-permute-start | bytes 387080 | tf_op jit(solution)/shard_map/ppermute | solution.py:385
  12.1 7.8 %collective-permute-start.1 = (f32[21,3,512]{2,1,0:T(4,128)}, f32[21,3,512]{2,1,0:T(4,128)}, u32[]{:S(2)}, u32[]{:S(2)}) collective-permute-start(f32[21,3,512]{2,1,0:T(4,128)} %pad_maximum_fusion.2), channel_id=1, source_target_pairs={{0,1},{1,2},{2,3},{3,4},{4,5},{5,6},{6,7},{7,8},{8,9},{9,10},{10,1... | collective-permute-start | bytes 387080 | tf_op jit(solution)/shard_map/ppermute | solution.py:388
  12.1 0.8 %copy-start.7 = (f32[16]{0:T(128)S(1)}, f32[16]{0:T(128)}, u32[]{:S(2)}) copy-start(f32[16]{0:T(128)} %param.12) | copy-start | bytes 196
  12.1 0.9 %copy-start.8 = (f32[10]{0:T(128)S(1)}, f32[10]{0:T(128)}, u32[]{:S(2)}) copy-start(f32[10]{0:T(128)} %param.14) | copy-start | bytes 124
  12.2 1.1 %copy-start.5 = (f32[16,243]{1,0:T(8,128)S(1)}, f32[16,243]{1,0:T(8,128)}, u32[]{:S(2)}) copy-start(f32[16,243]{1,0:T(8,128)} %param.11) | copy-start | bytes 46660
  12.4 8.7 %copy-start = (f32[256,1408]{1,0:T(8,128)S(1)}, f32[256,1408]{1,0:T(8,128)}, u32[]{:S(2)}) copy-start(f32[256,1408]{1,0:T(8,128)} %constant.13.clone.table_ref) | copy-start | bytes 4325380
  12.4 8.7 %copy-start.1 = (f32[4,4,8,512]{3,2,1,0:T(8,128)S(1)}, f32[4,4,8,512]{3,2,1,0:T(8,128)}, u32[]{:S(2)}) copy-start(f32[4,4,8,512]{3,2,1,0:T(8,128)} %links_ref.1) | copy-start | bytes 786436
  12.4 8.7 %copy-start.2 = (f32[4,4,8,512]{3,2,1,0:T(8,128)S(1)}, f32[4,4,8,512]{3,2,1,0:T(8,128)}, u32[]{:S(2)}) copy-start(f32[4,4,8,512]{3,2,1,0:T(8,128)} %cot_ref.1) | copy-start | bytes 786436
  12.4 8.7 %copy-start.3 = (s32[4]{0:T(128)S(1)}, s32[4]{0:T(128)}, u32[]{:S(2)}) copy-start(s32[4]{0:T(128)} %m_ref.1) | copy-start | bytes 52
  46.3 2.1 %copy-start.4 = (f32[16,1,256]{2,0,1:T(8,128)}, f32[16,1,256]{2,0,1:T(8,128)S(1)}, u32[]{:S(2)}) copy-start(f32[16,1,256]{2,0,1:T(8,128)S(1)} %copy.20) | copy-start | bytes 49156

commit v2 on v1

--- a/solution.py
+++ b/solution.py
@@ -210,7 +210,7 @@
     coeffs = dot3(head2, hidden2, NN) + hb_ref[...]
 
     row = lax.broadcasted_iota(jnp.int32, (ROWS, SITES), 0)
-    mask = jnp.concatenate([mask_ref[...], halo_ref[20]], axis=0)
+    mask = jnp.concatenate([mask_ref[...].astype(jnp.float32), halo_ref[20]], axis=0)
     inside = (row <= OWN) | (row >= ROWS - 2)
     chosen = (mask != 0.0) & inside
     active = tuple(
@@ -307,6 +307,42 @@
     return table
 
 
+def halo_kernel(
+    n, m_ref, links_ref, cot_ref, mask_ref, halo_ref,
+    head_ref, tail_ref, ahead_ref, behind_ref, send1, recv1, send2, recv2,
+):
+    me = lax.axis_index("ta")
+    after, before = lax.rem(me + 1, n), lax.rem(me + n - 1, n)
+    mesh_id = pl.DeviceIdType.MESH
+    barrier = pltpu.get_barrier_semaphore()
+    for neighbour in (before, after):
+        pl.semaphore_signal(barrier, inc=1, device_id={"ta": neighbour}, device_id_type=mesh_id)
+    m = m_ref[0]
+    for msg_ref, start in ((head_ref, 0), (tail_ref, OWN - REACH)):
+        rows = slice(start, start + REACH)
+        for c in range(4):
+            for d in range(4):
+                msg_ref[4 * d + c] = links_ref[d, c][rows]
+            msg_ref[16 + c] = cot_ref[m, c][rows]
+        msg_ref[20] = mask_ref[...].astype(jnp.float32)[rows]
+    pl.semaphore_wait(barrier, 2)
+    down = pltpu.make_async_remote_copy(
+        src_ref=head_ref, dst_ref=ahead_ref, send_sem=send1, recv_sem=recv1,
+        device_id={"ta": before}, device_id_type=mesh_id,
+    )
+    up = pltpu.make_async_remote_copy(
+        src_ref=tail_ref, dst_ref=behind_ref, send_sem=send2, recv_sem=recv2,
+        device_id={"ta": after}, device_id_type=mesh_id,
+    )
+    down.start()
+    up.start()
+    down.wait()
+    up.wait()
+    gap = jnp.zeros((ROWS - OWN - 2 * REACH, SITES), jnp.float32)
+    for c in range(21):
+        halo_ref[c] = jnp.concatenate([ahead_ref[c], gap, behind_ref[c]], axis=0)
+
+
 def sum_kernel(
     n, x_ref, out_ref, parts_ref, sums_ref, mine_ref, send1, recv1, send2, recv2
 ):
@@ -367,30 +403,19 @@
 def body(
     gauge_links, cotangent, conv_weight, conv_bias, head_weight, head_bias, site_mask, direction
 ):
-    active = direction[0]
-    mask = (site_mask != 0).astype(jnp.float32)
-    active_cot = lax.dynamic_index_in_dim(cotangent, active, 0, keepdims=False)
-
-    def message(rows):
-        return jnp.concatenate(
-            [
-                gauge_links[:, :, rows].reshape(16, REACH, SITES),
-                active_cot[:, rows],
-                mask[None, rows],
-            ],
-            axis=0,
-        )
-
     count = lax.axis_size("ta")
-    ahead = lax.ppermute(
-        message(slice(0, REACH)), "ta", [((i + 1) % count, i) for i in range(count)]
-    )
-    behind = lax.ppermute(
-        message(slice(OWN - REACH, OWN)), "ta", [(i, (i + 1) % count) for i in range(count)]
-    )
-    halo = jnp.concatenate(
-        [ahead, jnp.zeros((21, ROWS - OWN - 2 * REACH, SITES), jnp.float32), behind], axis=1
-    )
+    vmem = pl.BlockSpec(memory_space=pltpu.VMEM)
+    smem = pl.BlockSpec(memory_space=pltpu.SMEM)
+    f32, bf16 = jnp.float32, jnp.bfloat16
+    halo = pl.pallas_call(
+        partial(halo_kernel, count),
+        out_shape=jax.ShapeDtypeStruct((21, ROWS - OWN, SITES), f32),
+        in_specs=[smem, vmem, vmem, vmem],
+        out_specs=vmem,
+        scratch_shapes=[pltpu.VMEM((21, REACH, SITES), f32)] * 4
+        + [pltpu.SemaphoreType.DMA(())] * 4,
+        compiler_params=pltpu.CompilerParams(collective_id=1, has_side_effects=True),
+    )(direction, gauge_links, cotangent, site_mask)
 
     table = jnp.asarray(spread())
     weight = jnp.pad(conv_weight, ((0, 0), (0, PACK - AT_CB)))
@@ -401,15 +426,13 @@
     cb = jnp.tile(conv_bias, ROWS).reshape(ROWS * HID, 1)
     hb = jnp.repeat(head_bias, ROWS).reshape(COEF * ROWS, 1)
 
-    vmem = pl.BlockSpec(memory_space=pltpu.VMEM)
-    f32, bf16 = jnp.float32, jnp.bfloat16
     grad, packed = pl.pallas_call(
         partial(kernel, 1.0 / math.sqrt(count * OWN * SITES)),
         out_shape=(
             jax.ShapeDtypeStruct((4, 4, OWN, SITES), f32),
             jax.ShapeDtypeStruct((HID, PACK), f32),
         ),
-        in_specs=[pl.BlockSpec(memory_space=pltpu.SMEM)] + [vmem] * 9,
+        in_specs=[smem] + [vmem] * 9,
         out_specs=(vmem,) * 2,
         scratch_shapes=[
             pltpu.VMEM((GROUP, SITES), f32),
@@ -422,7 +445,7 @@
             pltpu.VMEM((BANK, SITES), f32),
         ],
         compiler_params=pltpu.CompilerParams(vmem_limit_bytes=40 * 2**20),
-    )(direction, gauge_links, halo, cotangent, mask, weight, table, head, cb, hb)
+    )(direction, gauge_links, halo, cotangent, site_mask, weight, table, head, cb, hb)
 
     depth = -(-HID // count)
     packed = jnp.pad(packed, ((0, count * depth - HID), (0, 0)))

time: 48.9 us -> 45.2 us (0.924)
  Pallas kernels: 23.8 us -> 37.7 us
  waiting for transfers between devices: 6.58 us -> 0 us
  starting transfers between devices: 5.45 us -> 0 us
  other arithmetic: 3.42 us -> 0.88 us
  between operations: 2.78 us -> 0.83 us
  local copies, waits for them, and re-layouts: 6.38 us -> 5.33 us
    pallas_call x0 -> x1, Pallas kernels: none -> 11.1 us  [body(): pl.pallas_call(partial(halo_kernel, count), out_shape=jax.ShapeDtypeStruc...]
    ppermute x2 -> x0, waiting for transfers between devices: 6.58 us -> none  [the longest x1 5.31 us: body(): lax.ppermute(message(slice(OWN - REACH, OWN)), 'ta', [(i, (i + 1) % count...]
    ppermute x2 -> x0, starting transfers between devices: 5.45 us -> none  [the longest x1 5.44 us: body(): lax.ppermute(message(slice(0, REACH)), 'ta', [((i + 1) % count, i) for i...]
    pallas_call x1, Pallas kernels: 10.7 us -> 13.9 us  [body(): pl.pallas_call(partial(sum_kernel, count), out_shape=jax.ShapeDtypeStruct...]
    concatenate x3 -> x0, other arithmetic: 2.52 us -> none  [the longest x2 1.41 us: message(): jnp.concatenate([gauge_links[:, :, rows].reshape(16, REACH, SITES), activ...]
    slice x2 -> x0, local copies, waits for them, and re-layouts: 1.09 us -> none  [the longest x1 1.08 us: message(): gauge_links[:, :, rows].reshape(16, REACH, SITES)]
    unnamed x20 -> x22, local copies, waits for them, and re-layouts: 1.45 us -> 2.43 us
    squeeze x1 -> x0, local copies, waits for them, and re-layouts: 0.85 us -> none  [body(): active_cot = lax.dynamic_index_in_dim(cotangent, active, 0, keepdims=False)]
  transfers between devices with their start and end apart: 2 -> 0, of which waited for: 2 -> 0; matrix products, arithmetic and copies ran while one was open for 4% -> 0% of each run, Pallas kernels for 0% -> 0%
where the time goes in v2:
time: 45.2 us; the launch traced here: 44.8 us
  Pallas kernels  37.7 us (83%)
  local copies, waits for them, and re-layouts  5.33 us (12%)
  other arithmetic  0.88 us (2%)
  between operations  0.83 us (2%)
    pallas_call x1, Pallas kernels, body(): pl.pallas_call(partial(sum_kernel, count), out_shape=jax.ShapeDtypeStruct...  13.9 us
    pallas_call x1, Pallas kernels, body(): pl.pallas_call(partial(kernel, 1.0 / math.sqrt(count * OWN * SITES)), out...  12.7 us
    pallas_call x1, Pallas kernels, body(): pl.pallas_call(partial(halo_kernel, count), out_shape=jax.ShapeDtypeStruc...  11.1 us
    unnamed x22, local copies, waits for them, and re-layouts  2.43 us

profile of v2, /device:TPU:0, one launch (start us, length us, event | category | flops | bytes accessed | tf_op | source)
XLA Modules:
  0.0 44.8 jit_solution(9659174916385490148)
XLA Ops:
  0.6 0.9 %broadcast_multiply_fusion = f32[10,16,16,16]{3,2,1,0:T(8,128)S(1)} fusion(f32[16,16]{1,0:T(8,128)S(1)} %fusion, f32[10,16]{1,0:T(8,128)} %param.13), kind=kLoop, calls=%fused_computation | loop fusion | flops 40960 | bytes 165504 | tf_op jit(solution)/shard_map/mul | solution.py:423
  1.5 0.0 copy-start.8
  1.5 0.0 copy-start.9
  1.6 0.0 copy-start.7
  1.6 0.0 copy-start
  1.6 0.0 copy-start.2
  1.6 0.0 copy-start.3
  1.6 0.0 copy-start.4
  1.6 0.0 copy-start.5
  1.6 0.6 %mul.20.head_ref = f32[160,256]{1,0:T(8,128)S(1)} reshape(f32[10,16,16,16]{3,2,1,0:T(8,128)S(1)} %broadcast_multiply_fusion) | data formatting | bytes 327680 | tf_op jit(solution)/shard_map/mul | solution.py:423
  2.2 11.1 %shard_map.128.halo_ref = f32[21,8,512]{2,1,0:T(8,128)} custom-call(s32[4]{0:T(128)} %m_ref.3, f32[4,4,8,512]{3,2,1,0:T(8,128)} %links_ref.3, f32[4,4,8,512]{3,2,1,0:T(8,128)} %cot_ref.3, s32[8,512]{1,0:T(8,128)} %mask_ref.3), custom_call_target="tpu_custom_call" | custom-call | tf_op jit(solution)/shard_map/pallas_call | solution.py:410
  13.3 0.0 copy-done.8
  13.3 0.1 reshape_tile.4.cb_ref
  13.4 0.0 copy-done.9
  13.4 0.1 broadcast_in_dim.2
  13.5 0.1 reshape_reshape.4.hb_ref
  13.6 0.0 copy-done.7
  13.6 0.0 copy-done
  13.6 0.0 copy-done.2
  13.7 0.0 copy-done.3
  13.7 0.0 copy-done.4
  13.7 0.0 copy-done.5
  13.7 0.0 copy-start.1
  13.7 1.0 %copy-done.1 = f32[21,8,512]{2,1,0:T(8,128)S(1)} copy-done((f32[21,8,512]{2,1,0:T(8,128)S(1)}, f32[21,8,512]{2,1,0:T(8,128)}, u32[]{:S(2)}) %copy-start.1) | copy-done | bytes 344088
  14.7 12.7 %shard_map.129 = (f32[4,4,8,512]{3,2,1,0:T(8,128)}, f32[16,256]{1,0:T(8,128)S(1)}) custom-call(s32[4]{0:T(128)S(1)} %copy-done.5, f32[4,4,8,512]{3,2,1,0:T(8,128)S(1)} %copy-done.2, f32[21,8,512]{2,1,0:T(8,128)S(1)} %copy-done.1, f32[4,4,8,512]{3,2,1,0:T(8,128)S(1)} %copy-done.3, s32[8,512]{1,0:T(8,128)S(1)} %copy-done.4, f32[16,256]{1,0:T(8,128)S(1)} %pad.4.cw_ref, ...), custom_call_target="tpu_custom_call" | custom-call | tf_op jit(solution)/shard_map/pallas_call | solution.py:429
  27.4 0.6 %reshape.30.x_ref = f32[16,1,256]{2,1,0:T(1,128)} reshape(f32[16,256]{1,0:T(8,128)S(1)} %get-tuple-element.8) | data formatting | bytes 32768 | tf_op jit(solution)/shard_map/reshape | solution.py:462
  28.0 13.9 %shard_map.130 = f32[16,1,256]{2,1,0:T(1,128)} custom-call(f32[16,1,256]{2,1,0:T(1,128)} %reshape.30.x_ref), custom_call_target="tpu_custom_call" | custom-call | tf_op jit(solution)/shard_map/pallas_call | solution.py:453
  41.9 0.7 %copy.20 = f32[16,1,256]{2,0,1:T(8,128)S(1)} copy(f32[16,1,256]{2,1,0:T(1,128)} %shard_map.130) | data formatting | bytes 32768
  42.6 0.1 slice_bitcast_fusion
  42.7 0.7 %copy.17 = f32[10,16]{1,0:T(8,128)} copy(f32[10,16]{0,1:T(8,128)S(1)} %slice_bitcast_fusion) | data formatting | bytes 1280
  43.4 0.7 %slice_reduce_fusion = f32[10]{0:T(128)} fusion(f32[16,256]{1,0:T(8,128)S(1)} %bitcast.9), kind=kLoop, calls=%fused_computation.2 | loop fusion | bytes 80 | tf_op jit(solution)/shard_map/slice | solution.py:469
  44.1 0.7 %slice_reduce_fusion.1 = f32[16]{0:T(128)} fusion(f32[16,256]{1,0:T(8,128)S(1)} %bitcast.10), kind=kLoop, calls=%fused_computation.4 | loop fusion | bytes 128 | tf_op jit(solution)/shard_map/slice | solution.py:467
  (5 shorter events, 0.0 us)
Async XLA Ops:
  1.5 11.8 %copy-start.8 = (f32[16]{0:T(128)S(1)}, f32[16]{0:T(128)}, u32[]{:S(2)}) copy-start(f32[16]{0:T(128)} %param.12) | copy-start | bytes 196
  1.5 11.9 %copy-start.9 = (f32[10]{0:T(128)S(1)}, f32[10]{0:T(128)}, u32[]{:S(2)}) copy-start(f32[10]{0:T(128)} %param.14) | copy-start | bytes 124
  1.6 12.1 %copy-start.7 = (f32[16,243]{1,0:T(8,128)S(1)}, f32[16,243]{1,0:T(8,128)}, u32[]{:S(2)}) copy-start(f32[16,243]{1,0:T(8,128)} %param.11) | copy-start | bytes 46660
  1.6 12.1 %copy-start = (f32[256,1408]{1,0:T(8,128)S(1)}, f32[256,1408]{1,0:T(8,128)}, u32[]{:S(2)}) copy-start(f32[256,1408]{1,0:T(8,128)} %constant.5.clone.table_ref) | copy-start | bytes 4325380
  1.6 12.1 %copy-start.2 = (f32[4,4,8,512]{3,2,1,0:T(8,128)S(1)}, f32[4,4,8,512]{3,2,1,0:T(8,128)}, u32[]{:S(2)}) copy-start(f32[4,4,8,512]{3,2,1,0:T(8,128)} %links_ref.3) | copy-start | bytes 786436
  1.6 12.1 %copy-start.3 = (f32[4,4,8,512]{3,2,1,0:T(8,128)S(1)}, f32[4,4,8,512]{3,2,1,0:T(8,128)}, u32[]{:S(2)}) copy-start(f32[4,4,8,512]{3,2,1,0:T(8,128)} %cot_ref.3) | copy-start | bytes 786436
  1.6 12.1 %copy-start.4 = (s32[8,512]{1,0:T(8,128)S(1)}, s32[8,512]{1,0:T(8,128)}, u32[]{:S(2)}) copy-start(s32[8,512]{1,0:T(8,128)} %mask_ref.3) | copy-start | bytes 49156
  1.6 12.1 %copy-start.5 = (s32[4]{0:T(128)S(1)}, s32[4]{0:T(128)}, u32[]{:S(2)}) copy-start(s32[4]{0:T(128)} %m_ref.3) | copy-start | bytes 52
  13.7 1.0 %copy-start.1 = (f32[21,8,512]{2,1,0:T(8,128)S(1)}, f32[21,8,512]{2,1,0:T(8,128)}, u32[]{:S(2)}) copy-start(f32[21,8,512]{2,1,0:T(8,128)} %shard_map.128.halo_ref) | copy-start | bytes 1032196
  42.6 2.1 %copy-start.6 = (f32[16,1,256]{2,0,1:T(8,128)}, f32[16,1,256]{2,0,1:T(8,128)S(1)}, u32[]{:S(2)}) copy-start(f32[16,1,256]{2,0,1:T(8,128)S(1)} %copy.20) | copy-start | bytes 49156
